TPU v7x, 512 devices: a whole 4x4x16 slice. The times are simulated.
512 devices in a mesh: dp: 4 (over y), gx: 4 (over z_hi), gy: 4 (over z_lo), gz: 8 (over x, core).
Axes of the slice: x: 4, y: 4, z: 16 (z_hi: 4, z_lo: 4; z = z_hi * 4 + z_lo), core: 2. Of those that a mesh axis runs over, the one named last changes fastest.
Arguments:
- inputs: bfloat16 [12288, 4096], P(('dp', 'gx', 'gz'), 'gy'), may hold values from -0.5 to 0.5
- out_grad: bfloat16 [12288, 14336], P(('dp', 'gx', 'gy'), 'gz'), may hold values from -6 to 6
- weight: bfloat16 [4096, 14336], P(('gy', 'gx'), 'gz'), may hold values from -0.09375 to 0.09375
Outputs:
- input_grad: bfloat16 [12288, 4096], P(('dp', 'gx', 'gz'), 'gy')
- weight_grad: bfloat16 [4096, 14336], P(('gy', 'gx'), 'gz')
All inputs are finite; a program needn't handle non-finite values.
Results may differ from a plain program's by a relative error of at most 0.017.
Values may be sent and summed in bfloat16 or wider, within the bound.
A program may use at most 64 MiB of HBM per device.

v0:
```python
import jax
import jax.numpy as jnp
from jax import lax
from jax.sharding import PartitionSpec as P


def per_device(inputs, out_grad, weight):
    grad_rows = lax.all_gather(out_grad, "gy", axis=0, tiled=True)
    terms = lax.dot_general(
        grad_rows,
        lax.all_gather(weight, "gx", axis=0, tiled=True),
        (((1,), (1,)), ((), ())),
        preferred_element_type=jnp.float32,
    )
    input_grad = lax.psum_scatter(terms.astype(jnp.bfloat16), "gz", scatter_dimension=0, tiled=True)
    groups = lax.axis_size("dp")
    blocks = lax.axis_size("gx")
    width = inputs.shape[1]
    hidden = out_grad.shape[1]
    total = lax.dot_general(
        lax.all_gather(inputs, "gz", axis=0, tiled=True),
        grad_rows,
        (((0,), (0,)), ((), ())),
        preferred_element_type=jnp.float32,
    )
    rounded = total.astype(jnp.bfloat16).reshape(blocks, width // blocks, hidden)
    received = lax.all_to_all(rounded, "gx", split_axis=0, concat_axis=0, tiled=True)
    summed = jnp.sum(received.astype(jnp.float32), axis=0)
    weight_grad = (lax.psum(summed.astype(jnp.bfloat16), "dp").astype(jnp.float32) / groups).astype(
        jnp.bfloat16
    )
    return (input_grad, weight_grad)


def solution(mesh):
    return jax.shard_map(
        per_device,
        mesh=mesh,
        in_specs=(P(("dp", "gx", "gz"), "gy"), P(("dp", "gx", "gy"), "gz"), P(("gy", "gx"), "gz")),
        out_specs=(P(("dp", "gx", "gz"), "gy"), P(("gy", "gx"), "gz")),
        check_vma=False,
    )
```

profile of v0, /device:TPU:8, one launch (start us, length us, event | category | flops | bytes accessed | tf_op | source)
XLA Modules:
  0.0 520.1 jit_solution(6062322387538755840)
XLA Ops:
  8.0 0.0 all-gather.8.cloned.1.call-start
  8.0 0.7 all-gather.8.cloned.1.call-update
  8.7 0.0 all-gather.4.cloned.1.call-start
  8.8 0.7 all-gather.4.cloned.1.call-update
  9.5 38.0 %all-gather.8.cloned.1.call-done = bf16[768,1024]{1,0:T(8,128)(2,1)} async-done(((bf16[96,1024]{1,0:T(8,128)(2,1)}), bf16[768,1024]{1,0:T(8,128)(2,1)}) %all-gather.8.cloned.1.call-update) | async-done | bytes 1572880 | tf_op jit(solution)/shard_map/all_gather | solution.py:21
  47.5 68.2 %all-gather.4.cloned.1.call-done = bf16[768,1792]{1,0:T(8,128)(2,1)} async-done(((bf16[192,1792]{1,0:T(8,128)(2,1)}), bf16[768,1792]{1,0:T(8,128)(2,1)}) %all-gather.4.cloned.1.call-update) | async-done | bytes 2752528 | tf_op jit(solution)/shard_map/all_gather | solution.py:8
  115.7 7.1 %convolution_convert_fusion = bf16[1024,1792]{1,0:T(8,128)(2,1)} fusion(bf16[768,1024]{1,0:T(8,128)(2,1)} %all-gather.8.cloned.1.call-done, bf16[768,1792]{1,0:T(8,128)(2,1)} %all-gather.4.cloned.1.call-done), kind=kOutput, calls=%fused_computation | convolution fusion | flops 2820407296 | bytes 7995392 | tf_op jit(solution)/shard_map/dot_general | solution.py:20
  122.9 10.6 %all-to-all-start = ((bf16[4,256,1792]{2,1,0:T(8,128)(2,1)}), bf16[4,256,1792]{2,1,0:T(8,128)(2,1)}, u32[]{:S(2)}, u32[]{:S(2)}) async-start(bf16[4,256,1792]{2,1,0:T(8,128)(2,1)} %bitcast.5), calls=%async_computation.1 | async-start | bytes 7340032 | tf_op jit(solution)/shard_map/all_to_all | solution.py:27
  133.5 0.0 all-gather.6.cloned.1.call-start
  133.5 0.6 all-gather.6.cloned.1.call-update
  134.0 0.0 copy-start
  134.0 0.0 all-reduce.2.cloned.1.call-start
  134.1 260.4 %all-to-all-done = bf16[4,256,1792]{2,1,0:T(8,128)(2,1)} async-done(((bf16[4,256,1792]{2,1,0:T(8,128)(2,1)}), bf16[4,256,1792]{2,1,0:T(8,128)(2,1)}, u32[]{:S(2)}, u32[]{:S(2)}) %all-to-all-start) | async-done | bytes 3670048 | tf_op jit(solution)/shard_map/all_to_all | solution.py:27
  394.5 3.8 reduce_sum.12
  398.2 0.0 all-reduce.2.cloned.1.call-update
  398.3 0.0 reduce-scatter.2.cloned.1.call-start
  398.3 21.6 %all-gather.6.cloned.1.call-done = bf16[1024,1792]{1,0:T(8,128)(2,1)} async-done(((bf16[256,1792]{1,0:T(8,128)(2,1)}), bf16[1024,1792]{1,0:T(8,128)(2,1)}) %all-gather.6.cloned.1.call-update) | async-done | bytes 3670032 | tf_op jit(solution)/shard_map/all_gather | solution.py:11
  419.9 0.0 copy-done
  419.9 6.2 %convolution_convert_fusion.1 = bf16[768,1024]{1,0:T(8,128)(2,1)} fusion(bf16[768,1792]{1,0:T(8,128)(2,1)S(1)} %copy-done, bf16[1024,1792]{1,0:T(8,128)(2,1)} %all-gather.6.cloned.1.call-done), kind=kOutput, calls=%fused_computation.2 | convolution fusion | flops 2819358720 | bytes 7995392 | tf_op jit(solution)/shard_map/dot_general | solution.py:9
  426.0 0.0 reduce-scatter.2.cloned.1.call-update
  426.1 41.9 %all-reduce.2.cloned.1.call-done = bf16[256,1792]{1,0:T(8,128)(2,1)} async-done(((bf16[256,1792]{1,0:T(8,128)(2,1)}), bf16[256,1792]{1,0:T(8,128)(2,1)}) %all-reduce.2.cloned.1.call-update) | async-done | bytes 917520 | tf_op jit(solution)/shard_map/psum | solution.py:29
  468.0 2.2 multiply_convert_fusion
  470.2 42.7 %reduce-scatter.2.cloned.1.call-done = bf16[96,1024]{1,0:T(8,128)(2,1)} async-done(((bf16[768,1024]{1,0:T(8,128)(2,1)}), bf16[96,1024]{1,0:T(8,128)(2,1)}) %reduce-scatter.2.cloned.1.call-update) | async-done | bytes 196624 | tf_op jit(solution)/shard_map/reduce_scatter | solution.py:15
Async XLA Ops:
  8.0 39.5 %all-gather.8.cloned.1.call-start = ((), (), s32[]{:S(2)}) async-start(), calls=%async_computation.5 | async-start | bytes 1769472 | tf_op jit(solution)/shard_map/all_gather | solution.py:21
  8.7 107.0 %all-gather.4.cloned.1.call-start = ((), (), s32[]{:S(2)}) async-start(), calls=%async_computation.2 | async-start | bytes 3440640 | tf_op jit(solution)/shard_map/all_gather | solution.py:8
  122.9 271.6 %all-to-all-start = ((bf16[4,256,1792]{2,1,0:T(8,128)(2,1)}), bf16[4,256,1792]{2,1,0:T(8,128)(2,1)}, u32[]{:S(2)}, u32[]{:S(2)}) async-start(bf16[4,256,1792]{2,1,0:T(8,128)(2,1)} %bitcast.5), calls=%async_computation.1 | async-start | bytes 7340032 | tf_op jit(solution)/shard_map/all_to_all | solution.py:27
  133.5 286.4 %all-gather.6.cloned.1.call-start = ((), (), s32[]{:S(2)}) async-start(), calls=%async_computation.3 | async-start | bytes 4587520 | tf_op jit(solution)/shard_map/all_gather | solution.py:11
  134.0 285.9 %copy-start = (bf16[768,1792]{1,0:T(8,128)(2,1)S(1)}, bf16[768,1792]{1,0:T(8,128)(2,1)}, u32[]{:S(2)}) copy-start(bf16[768,1792]{1,0:T(8,128)(2,1)} %all-gather.4.cloned.1.call-done) | copy-start | bytes 8257540
  134.0 334.0 %all-reduce.2.cloned.1.call-start = ((), (), s32[]{:S(2)}) async-start(), calls=%async_computation.6 | async-start | bytes 1835008 | tf_op jit(solution)/shard_map/psum | solution.py:29
  398.3 114.7 %reduce-scatter.2.cloned.1.call-start = ((), (), s32[]{:S(2)}) async-start(), calls=%async_computation.4 | async-start | bytes 1769472 | tf_op jit(solution)/shard_map/reduce_scatter | solution.py:15
Sparse Core Ops, SparseCore 0:
  11.0 36.5 all-gather.7
  49.6 66.0 all-gather.3
  398.4 69.5 all-reduce.1
  471.3 41.6 reduce-scatter.1
Sparse Core Ops, SparseCore 1:
  136.0 283.8 all-gather.5
where the time goes:
time: 520 us
  waiting for transfers between devices  475 us (91%)
  between operations  15.2 us (3%)
  matrix products  13.3 us (3%)
  starting transfers between devices  10.7 us (2%)
  other arithmetic  6 us (1%)
    all_to_all x1, waiting for transfers between devices, per_device(): lax.all_to_all(rounded, 'gx', split_axis=0, concat_axis=0, tiled=True)  260 us
    all_gather x1, waiting for transfers between devices, per_device(): grad_rows = lax.all_gather(out_grad, 'gy', axis=0, tiled=True)  68.2 us
    reduce_scatter x1, waiting for transfers between devices, per_device(): lax.psum_scatter(terms.astype(jnp.bfloat16), 'gz', scatter_dimension=0, t...  42.7 us
    psum x1, waiting for transfers between devices, per_device(): lax.psum(summed.astype(jnp.bfloat16), 'dp').astype(jnp.float32) / groups  41.9 us
    all_gather x1, waiting for transfers between devices, per_device(): lax.all_gather(inputs, 'gz', axis=0, tiled=True)  38 us
    all_gather x1, waiting for transfers between devices, per_device(): lax.all_gather(weight, 'gx', axis=0, tiled=True)  21.6 us
    all_to_all x1, starting transfers between devices, per_device(): lax.all_to_all(rounded, 'gx', split_axis=0, concat_axis=0, tiled=True)  10.6 us
  transfers between devices with their start and end apart: 6, of which 6 were waited for; matrix products, arithmetic and copies ran while one was open for 2% of the time, Pallas kernels for 0%

commit v1 on v0

v1 whole, which is shorter than its diff:
```python
import jax
import jax.numpy as jnp
from jax import lax
from jax.sharding import PartitionSpec as P


def per_device(inputs, out_grad, weight):
    groups = lax.axis_size("dp")
    blocks = lax.axis_size("gx")
    width = inputs.shape[1]
    rows, hidden = weight.shape
    part = rows // groups

    own = lax.dynamic_slice_in_dim(weight, lax.axis_index("dp") * part, part, 0)
    own = lax.all_gather(own, "gx", axis=0, tiled=False)
    whole = lax.all_gather(own, "dp", axis=1, tiled=False).reshape(width, hidden)
    grad_rows = lax.all_gather(out_grad, "gy", axis=0, tiled=True)
    total = lax.dot_general(
        lax.all_gather(inputs, "gz", axis=0, tiled=True),
        grad_rows,
        (((0,), (0,)), ((), ())),
        preferred_element_type=jnp.float32,
    )
    rounded = total.astype(jnp.bfloat16).reshape(blocks, groups, part, hidden)
    summed = lax.psum_scatter(rounded, "dp", scatter_dimension=1, tiled=False)
    summed = lax.psum_scatter(summed, "gx", scatter_dimension=0, tiled=False)
    summed = (summed.astype(jnp.float32) / groups).astype(jnp.bfloat16)
    weight_grad = lax.all_gather(summed, "dp", axis=0, tiled=True)

    terms = lax.dot_general(
        grad_rows,
        whole,
        (((1,), (1,)), ((), ())),
        preferred_element_type=jnp.float32,
    )
    input_grad = lax.psum_scatter(terms.astype(jnp.bfloat16), "gz", scatter_dimension=0, tiled=True)
    return (input_grad, weight_grad)


def solution(mesh):
    return jax.shard_map(
        per_device,
        mesh=mesh,
        in_specs=(P(("dp", "gx", "gz"), "gy"), P(("dp", "gx", "gy"), "gz"), P(("gy", "gx"), "gz")),
        out_specs=(P(("dp", "gx", "gz"), "gy"), P(("gy", "gx"), "gz")),
        check_vma=False,
    )
```

time: 520 us -> 331 us (0.64)
  waiting for transfers between devices: 475 us -> 244 us
  blocking collectives: 0 us -> 55.4 us
  starting transfers between devices: 10.7 us -> 0.24 us
    all_to_all x1 -> x0, waiting for transfers between devices: 260 us -> none  [per_device(): lax.all_to_all(rounded, 'gx', split_axis=0, concat_axis=0, tiled=True)]
    all_gather x0 -> x2, blocking collectives: none -> 55.4 us  [the longest x1 41.2 us: per_device(): own = lax.all_gather(own, 'gx', axis=0, tiled=False)]
    psum x1 -> x0, waiting for transfers between devices: 41.9 us -> none  [per_device(): lax.psum(summed.astype(jnp.bfloat16), 'dp').astype(jnp.float32) / groups]
    all_gather x1, waiting for transfers between devices: 21.6 us -> 53.8 us  [per_device(): lax.all_gather(own, 'dp', axis=1, tiled=False).reshape(width, hidden)]
    unnamed x5 -> x7, waiting for transfers between devices: 1.96 us -> 24.1 us
    reduce_scatter x1 -> x2, waiting for transfers between devices: 42.7 us -> 59.7 us  [the longest x1 52 us: per_device(): summed = lax.psum_scatter(summed, 'gx', scatter_dimension=0, tiled=False)]
    all_to_all x1 -> x0, starting transfers between devices: 10.6 us -> none  [per_device(): lax.all_to_all(rounded, 'gx', split_axis=0, concat_axis=0, tiled=True)]
  transfers between devices with their start and end apart: 6 -> 6, of which waited for: 6 -> 6; matrix products, arithmetic and copies ran while one was open for 2% -> 3% of each run, Pallas kernels for 0% -> 0%
where the time goes in v1:
time: 331 us
  waiting for transfers between devices  244 us (74%)
  blocking collectives  55.4 us (17%)
  between operations  14.2 us (4%)
  matrix products  11.3 us (3%)
  local copies, waits for them, and re-layouts  4.73 us (1%)
    all_gather x1, waiting for transfers between devices, per_device(): grad_rows = lax.all_gather(out_grad, 'gy', axis=0, tiled=True)  68.2 us
    all_gather x1, waiting for transfers between devices, per_device(): lax.all_gather(own, 'dp', axis=1, tiled=False).reshape(width, hidden)  53.8 us
    reduce_scatter x1, waiting for transfers between devices, per_device(): summed = lax.psum_scatter(summed, 'gx', scatter_dimension=0, tiled=False)  52 us
    all_gather x1, blocking collectives, per_device(): own = lax.all_gather(own, 'gx', axis=0, tiled=False)  41.2 us
    all_gather x1, waiting for transfers between devices, per_device(): lax.all_gather(inputs, 'gz', axis=0, tiled=True)  38 us
    unnamed x7, waiting for transfers between devices  24.1 us
    all_gather x1, blocking collectives, per_device(): weight_grad = lax.all_gather(summed, 'dp', axis=0, tiled=True)  14.2 us
    reduce_scatter x1, waiting for transfers between devices, per_device(): summed = lax.psum_scatter(rounded, 'dp', scatter_dimension=1, tiled=False)  7.66 us
  transfers between devices with their start and end apart: 6, of which 6 were waited for; matrix products, arithmetic and copies ran while one was open for 3% of the time, Pallas kernels for 0%

profile of v1, /device:TPU:8, one launch (start us, length us, event | category | flops | bytes accessed | tf_op | source)
XLA Modules:
  0.0 330.6 jit_solution(16499832434805265239)
XLA Ops:
  7.2 0.0 all-gather.9.cloned.1.call-start
  7.2 0.7 all-gather.9.cloned.1.call-update
  7.9 0.0 all-gather.7.cloned.1.call-start
  8.0 0.7 all-gather.7.cloned.1.call-update
  8.7 0.0 reduce-scatter.6.cloned.1.call-start
  8.7 38.0 %all-gather.9.cloned.1.call-done = bf16[768,1024]{1,0:T(8,128)(2,1)} async-done(((bf16[96,1024]{1,0:T(8,128)(2,1)}), bf16[768,1024]{1,0:T(8,128)(2,1)}) %all-gather.9.cloned.1.call-update) | async-done | bytes 1572880 | tf_op jit(solution)/shard_map/all_gather | solution.py:19
  46.7 68.2 %all-gather.7.cloned.1.call-done = bf16[768,1792]{1,0:T(8,128)(2,1)} async-done(((bf16[192,1792]{1,0:T(8,128)(2,1)}), bf16[768,1792]{1,0:T(8,128)(2,1)}) %all-gather.7.cloned.1.call-update) | async-done | bytes 2752528 | tf_op jit(solution)/shard_map/all_gather | solution.py:17
  114.9 5.3 %convolution_convert_fusion = bf16[1024,1792]{1,0:T(8,128)(2,1)S(1)} fusion(bf16[768,1024]{1,0:T(8,128)(2,1)} %all-gather.9.cloned.1.call-done, bf16[768,1792]{1,0:T(8,128)(2,1)} %all-gather.7.cloned.1.call-done), kind=kOutput, calls=%fused_computation | convolution fusion | flops 2820407296 | bytes 7995392 | tf_op jit(solution)/shard_map/dot_general | solution.py:18
  120.3 2.1 copy.7
  122.4 0.0 reduce-scatter.6.cloned.1.call-update
  122.4 0.0 all-gather.11.cloned.1.call-start
  122.5 41.2 %all-gather = bf16[256,1792]{1,0:T(8,128)(2,1)} all-gather(bf16[64,1792]{1,0:T(8,128)(2,1)S(1)} %constant_dynamic-slice_fusion), channel_id=2, replica_groups=mesh['dp'=4,'gx'=4,'gy'=4,'gz'=8] {'gx'}, dimensions={0}, use_global_device_ids=true | all-gather | bytes 1146880 | tf_op jit(solution)/shard_map/all_gather | solution.py:15
  163.7 0.0 all-gather.11.cloned.1.call-update
  163.8 0.0 reduce-scatter.8.cloned.1.call-start
  163.8 7.7 %reduce-scatter.6.cloned.1.call-done = bf16[4,1,64,1792]{3,2,0,1:T(8,128)(2,1)} async-done(((bf16[4,4,64,1792]{3,2,0,1:T(8,128)(2,1)}), bf16[4,1,64,1792]{3,2,0,1:T(8,128)(2,1)}) %reduce-scatter.6.cloned.1.call-update) | async-done | bytes 917520 | tf_op jit(solution)/shard_map/reduce_scatter | solution.py:25
  171.5 0.0 reduce-scatter.10.cloned.1.call-start
  171.5 53.8 %all-gather.11.cloned.1.call-done = bf16[4,256,1792]{2,1,0:T(8,128)(2,1)} async-done(((bf16[4,64,1792]{2,1,0:T(8,128)(2,1)}), bf16[4,256,1792]{2,1,0:T(8,128)(2,1)}) %all-gather.11.cloned.1.call-update) | async-done | bytes 3670032 | tf_op jit(solution)/shard_map/all_gather | solution.py:16
  225.4 5.9 %fusion = bf16[768,1024]{0,1:T(8,128)(2,1)S(1)} fusion(bf16[1024,1792]{1,0:T(8,128)(2,1)} %bitcast.16, bf16[768,1792]{1,0:T(8,128)(2,1)} %all-gather.7.cloned.1.call-done), kind=kOutput, calls=%fused_computation.2 | convolution fusion | flops 2819358720 | bytes 7995392 | tf_op jit(solution)/shard_map/dot_general | solution.py:30
  231.3 1.7 copy.9
  233.0 52.0 %reduce-scatter.8.cloned.1.call-done = bf16[1,64,1792]{2,1,0:T(8,128)(2,1)} async-done(((bf16[4,64,1792]{2,1,0:T(8,128)(2,1)}), bf16[1,64,1792]{2,1,0:T(8,128)(2,1)}) %reduce-scatter.8.cloned.1.call-update) | async-done | bytes 229392 | tf_op jit(solution)/shard_map/reduce_scatter | solution.py:26
  285.0 1.0 multiply_convert_fusion
  286.0 14.2 %all-gather.2 = bf16[1,256,1792]{2,1,0:T(8,128)(2,1)S(1)} all-gather(bf16[1,64,1792]{2,1,0:T(8,128)(2,1)S(1)} %multiply_convert_fusion), channel_id=4, replica_groups=mesh['dp'=4,'gx'=4,'gy'=4,'gz'=8] {'dp'}, dimensions={1}, use_global_device_ids=true | all-gather | bytes 1146880 | tf_op jit(solution)/shard_map/all_gather | solution.py:28
  300.2 22.6 %reduce-scatter.10.cloned.1.call-done = bf16[96,1024]{1,0:T(8,128)(2,1)} async-done(((bf16[768,1024]{1,0:T(8,128)(2,1)}), bf16[96,1024]{1,0:T(8,128)(2,1)}) %reduce-scatter.10.cloned.1.call-update) | async-done | bytes 196624
  322.8 0.9 copy.12
  (5 shorter events, 0.1 us)
Async XLA Ops:
  7.2 115.3 %copy-start = (bf16[256,1792]{1,0:T(8,128)(2,1)S(1)}, bf16[256,1792]{1,0:T(8,128)(2,1)}, u32[]{:S(2)}) copy-start(bf16[256,1792]{1,0:T(8,128)(2,1)} %param.5) | copy-start | bytes 2752516
  7.2 39.5 %all-gather.9.cloned.1.call-start = ((), (), s32[]{:S(2)}) async-start(), calls=%async_computation.4 | async-start | bytes 1769472 | tf_op jit(solution)/shard_map/all_gather | solution.py:19
  7.9 107.0 %all-gather.7.cloned.1.call-start = ((), (), s32[]{:S(2)}) async-start(), calls=%async_computation.3 | async-start | bytes 3440640 | tf_op jit(solution)/shard_map/all_gather | solution.py:17
  8.7 162.8 %reduce-scatter.6.cloned.1.call-start = ((), (), s32[]{:S(2)}) async-start(), calls=%async_computation.5 | async-start | bytes 4587520 | tf_op jit(solution)/shard_map/reduce_scatter | solution.py:25
  122.4 103.0 %all-gather.11.cloned.1.call-start = ((), (), s32[]{:S(2)}) async-start(), calls=%async_computation.7 | async-start | bytes 4587520 | tf_op jit(solution)/shard_map/all_gather | solution.py:16
  163.8 121.3 %reduce-scatter.8.cloned.1.call-start = ((), (), s32[]{:S(2)}) async-start(), calls=%async_computation.6 | async-start | bytes 1146880 | tf_op jit(solution)/shard_map/reduce_scatter | solution.py:26
  171.5 151.3 %reduce-scatter.10.cloned.1.call-start = ((), (), s32[]{:S(2)}) async-start(), calls=%async_computation.8 | async-start | bytes 1769472
Sparse Core Ops, SparseCore 0:
  10.1 36.5 all-gather.8
  48.8 66.0 all-gather.6
  122.5 48.8 reduce-scatter.5
  173.4 51.9 all-gather.10
  228.1 56.9 reduce-scatter.7
  288.3 34.4 reduce-scatter.9

commit v2 on v0

v2 whole, which is shorter than its diff:
```python
import functools

import jax
import jax.numpy as jnp
from jax import lax
from jax.experimental import pallas as pl
from jax.experimental.pallas import tpu as pltpu
from jax.sharding import PartitionSpec as P

MESH = pl.DeviceIdType.MESH
NC = 8
HOP = 2
START = 12
BF16, F32 = jnp.bfloat16, jnp.float32


def kernel(
    inp, og, wt, ig_out, wg_out,
    G, W, X, I1, PT, RD, T, CT, S, XR, R, Q, O, FB,
    wr, ws, dr, dss, yr, ysd, gr, gs, g2r, g2s, s1r, s1s, s2r, s2s, s3r, s3s, s4r, s4s,
    ctr, cts, xrr, xrs, qr, qs, orr, ors, loc,
):
    y, h, zl = lax.axis_index("dp"), lax.axis_index("gx"), lax.axis_index("gy")
    gz = lax.axis_index("gz")
    x, c = gz // 2, gz % 2
    z = h * 4 + zl
    r = (zl - y + 4) % 4
    tok = og.shape[0] // 2
    half = 4 * tok
    quarter = inp.shape[1] // 4
    rows = wt.shape[0] // NC

    def zdev(zz):
        return {"gx": zz // 4, "gy": zz % 4}

    def xdev(xx):
        return {"gz": xx * 2 + c}

    right = (zdev((z + 1) % 16), zdev((z + 15) % 16))
    ydev = ({"dp": (y + 1) % 4}, {"dp": (y + 3) % 4})
    core = {"gz": x * 2 + 1 - c}
    rd = (r, (4 - r) % 4)
    rr = tuple(jnp.where(v == 0, 4, v) for v in rd)
    sign = (1, -1)

    def held_from(d, cls):
        return ((z - sign[d] * (rd[d] + 4 * cls) + 32) % 16) // 4

    def bound_for(d, s):
        return ((z + sign[d] * (4 - rd[d] + 4 * (1 - s)) + 32) % 16) // 4

    def in_half(d, i):
        return i < NC // 2 if d == 0 else i >= NC // 2

    def remote(src, dst, send, recv, dev):
        return pltpu.make_async_remote_copy(
            src_ref=src, dst_ref=dst, send_sem=send, recv_sem=recv, device_id=dev, device_id_type=MESH
        )

    def tokens(first):
        return pl.ds(pl.multiple_of(first, 32), tok)

    def halves(which):
        return pl.ds(pl.multiple_of(which * half, 128), half)

    def chunk(i):
        return pl.ds(pl.multiple_of(i * rows, rows), rows)

    def columns(q):
        return pl.ds(pl.multiple_of(q * quarter, 128), quarter)

    def w_copy(d, stream, i):
        part = W.at[held_from(d, stream), chunk(i)]
        return remote(part, part, ws.at[d, stream, i], wr.at[d, stream, i], right[d])

    def d_copy(d, s, i):
        to = s + jnp.where(rd[d] == 3, 1, 0)
        return remote(RD.at[d, s, chunk(i)], RD.at[d, to, chunk(i)], dss.at[d, s, i], dr.at[d, s, i], right[d])

    def y_copy(d, i):
        return remote(FB.at[chunk(i)], FB.at[chunk(i)], ysd.at[d, i], yr.at[i], ydev[d])

    def g_copy(d, k):
        part = G.at[tokens(k * half + y * tok)]
        return remote(part, part, gs.at[d, k], gr.at[d, k], ydev[d])

    def g2_copy(d):
        part = G.at[tokens(d * half + ((y + 3 + 2 * d) % 4) * tok)]
        return remote(part, part, g2s.at[d], g2r.at[d], ydev[d])

    def s1_copy(dx):
        to = (x + dx) % 4
        return remote(inp.at[:, columns(to)], I1.at[x], s1s.at[dx], s1r.at[x], xdev(to))

    def s2_copy(t):
        j = (zl + t) % 4
        return remote(I1.at[j], X.at[x, tokens(c * half + y * tok)], s2s.at[t], s2r.at[y], {"dp": zl, "gy": j})

    def s3_copy(dx):
        part = X.at[x, halves(c)]
        return remote(part, part, s3s.at[dx], s3r.at[x], xdev((x + dx) % 4))

    def s4_copy(g):
        part = X.at[g, halves(c)]
        return remote(part, part, s4s.at[g], s4r.at[g], core)

    def ct_copy(g):
        return remote(T.at[g, halves(1 - c)], CT.at[g], cts.at[g], ctr.at[g], core)

    def xr_copy(dx):
        to = (x + dx) % 4
        return remote(S.at[to], XR.at[x], xrs.at[dx], xrr.at[x], xdev(to))

    def q_copy(t):
        k = (y + t) % 4
        return remote(R.at[tokens(k * tok)], Q.at[zl], qs.at[t], qr.at[zl], {"dp": k, "gy": y})

    def o_copy(dx):
        to = (x + dx) % 4
        return remote(Q.at[to], O.at[x], ors.at[dx], orr.at[x], xdev(to))

    def arrived(dst, send, recv, dev):
        remote(dst, dst, send, recv, dev).wait_recv()

    barrier = pltpu.get_barrier_semaphore()

    def greet(dev):
        pl.semaphore_signal(barrier, inc=1, device_id=dev, device_id_type=MESH)

    for dev in (*right, *ydev, core):
        greet(dev)
    for dx in (1, 2, 3):
        greet(xdev((x + dx) % 4))
    for t in (1, 2, 3):
        greet({"dp": zl, "gy": (zl + t) % 4})
        greet({"dp": (y + t) % 4, "gy": y})

    @pl.when(r != 0)
    def _():
        greet({"dp": zl, "gy": zl})
        greet({"dp": y, "gy": y})

    own = [
        pltpu.make_async_copy(og.at[pl.ds(k * tok, tok)], G.at[tokens(k * half + y * tok)], loc.at[k]) for k in (0, 1)
    ]
    own.append(pltpu.make_async_copy(inp.at[:, columns(x)], I1.at[x], loc.at[2]))
    for copy in own:
        copy.start()

    @pl.when(r == 0)
    def _():
        held = pltpu.make_async_copy(wt, W.at[h], loc.at[3])
        held.start()
        held.wait()

    for copy in own:
        copy.wait()
    pl.semaphore_wait(barrier, jnp.where(r == 0, 14, 16))

    for dx in (1, 2, 3):
        s1_copy(dx).start()
    for k in (0, 1):
        g_copy(0, k).start()
        g_copy(1, 1 - k).start()

    @pl.when(r == 0)
    def _():
        def first(i, _):
            w_copy(0, 0, i).start()
            w_copy(1, 0, i).start()
            return 0

        lax.fori_loop(0, NC, first, 0)

    def w_step(d, s):
        m = s - HOP * rr[d]

        @pl.when((m >= 0) & (m < 2 * NC))
        def _():
            stream, i = m // NC, m % NC
            cls = stream + jnp.where(rd[d] == 0, 1, 0)

            @pl.when((cls < 2) | in_half(d, i))
            def _():
                part = W.at[held_from(d, cls), chunk(i)]
                arrived(part, ws.at[d, 0, 0], wr.at[d, stream, i], right[d])

            @pl.when((cls == 0) | ((cls == 1) & ((rd[d] != 3) | in_half(d, i))))
            def _():
                w_copy(d, cls, i).start()

    def add(d, s, i, received):
        own_term = PT[bound_for(d, s), chunk(i), :]
        if received:
            own_term = own_term + RD[d, s, chunk(i), :].astype(F32)
        RD[d, s, chunk(i), :] = own_term.astype(BF16)
        d_copy(d, s, i).start()

    def d_step(d, s):
        @pl.when((rd[d] == 0) & (s >= 0) & (s < NC))
        def _():
            @pl.when(in_half(d, s))
            def _():
                add(d, 0, s, False)

        m = s - HOP * rr[d]

        @pl.when((m >= 0) & (m < 2 * NC))
        def _():
            stream, i = m // NC, m % NC
            slot = stream + jnp.where(rd[d] == 0, 1, 0)
            expected = (slot > 0) | (rd[d] > 1) | in_half(d, i)

            @pl.when(expected)
            def _():
                arrived(RD.at[d, slot, chunk(i)], dss.at[d, 0, 0], dr.at[d, stream, i], right[d])

            @pl.when((slot < 2) & expected)
            def _():
                add(d, slot, i, True)

            @pl.when((slot < 2) & jnp.logical_not(expected))
            def _():
                add(d, slot, i, False)

    groups = 4

    def last_step(s):
        i = s - HOP * 4 - NC

        @pl.when((r == 0) & (i >= 0) & (i < NC))
        def _():
            total = PT[h, chunk(i), :] + RD[0, 2, chunk(i), :].astype(F32) + RD[1, 2, chunk(i), :].astype(F32)
            mean = (total / groups).astype(BF16)
            FB[chunk(i), :] = mean
            wg_out[chunk(i), :] = mean
            y_copy(0, i).start()
            y_copy(1, i).start()

        away = rd[1]
        n = i - HOP * jnp.where(away == 2, 2, 1)

        @pl.when((r != 0) & (n >= 0) & (n < NC))
        def _():
            arrived(FB.at[chunk(n)], ysd.at[0, 0], yr.at[n], ydev[0])

            @pl.when((away == 1) & (n % 2 == 0))
            def _():
                y_copy(0, n).start()

            @pl.when((away == 3) & (n % 2 == 1))
            def _():
                y_copy(1, n).start()

            wg_out[chunk(n), :] = FB[chunk(n), :]

    def in_places():
        for dx in (1, 2, 3):
            j = (x + dx) % 4
            arrived(I1.at[j], s1s.at[0], s1r.at[j], core)

        @pl.when(r == 0)
        def _():
            mine = pltpu.make_async_copy(I1.at[zl], X.at[x, tokens(c * half + y * tok)], loc.at[3])
            mine.start()
            mine.wait()

        @pl.when(r != 0)
        def _():
            s2_copy(0).start()

        for t in (1, 2, 3):
            s2_copy(t).start()

    def grad_relay():
        for d in (0, 1):
            k = (y + 3 + 2 * d) % 4
            arrived(G.at[tokens(d * half + k * tok)], gs.at[0, 0], gr.at[d, d], core)
            g2_copy(d).start()

    def in_spread():
        for t in (0, 1, 2, 3):
            k = (y + t) % 4

            def wait(k=k):
                arrived(X.at[x, tokens(c * half + k * tok)], s2s.at[0], s2r.at[k], core)

            if t == 0:
                pl.when(r != 0)(wait)
            else:
                wait()
        for dx in (1, 2, 3):
            s3_copy(dx).start()
        s4_copy(x).start()

    def in_cores():
        for dx in (1, 2, 3):
            g = (x + dx) % 4
            arrived(X.at[g, halves(c)], s3s.at[0], s3r.at[g], core)
            s4_copy(g).start()

    def in_done():
        for g in range(4):
            arrived(X.at[g, halves(1 - c)], s4s.at[0], s4r.at[g], core)
        for d in (0, 1):
            k = (y + 3 + 2 * d) % 4
            arrived(G.at[tokens((1 - d) * half + k * tok)], gs.at[0, 0], gr.at[d, 1 - d], core)
            k = (y + 2) % 4
            arrived(G.at[tokens(d * half + k * tok)], g2s.at[0], g2r.at[d], core)

    def p_job(g):
        def tile(n, _):
            cols = pl.ds(pl.multiple_of(n * 256, 256), 256)
            PT[g, :, cols] = lax.dot_general(
                X[g], G[:, cols], (((0,), (0,)), ((), ())), preferred_element_type=F32
            )
            return 0

        lax.fori_loop(0, G.shape[1] // 256, tile, 0)

    def t_job(g):
        def part(n, _):
            where = halves((1 - c + n) % 2)
            T[g, where, :] = lax.dot_general(
                G[where, :], W[g], (((1,), (1,)), ((), ())), preferred_element_type=F32
            ).astype(BF16)

            @pl.when(n == 0)
            def _():
                ct_copy(g).start()

            return 0

        lax.fori_loop(0, 2, part, 0)

    def cores_sum(g):
        arrived(CT.at[g], cts.at[0], ctr.at[g], core)
        S[g] = (T[g, halves(c), :].astype(F32) + CT[g].astype(F32)).astype(BF16)

    def x_send():
        for g in range(4):
            cores_sum(g)
        for dx in (1, 2, 3):
            xr_copy(dx).start()

    def x_sum():
        total = S[x].astype(F32)
        for dx in (1, 2, 3):
            g = (x + dx) % 4
            arrived(XR.at[g], xrs.at[0], xrr.at[g], core)
            total = total + XR[g].astype(F32)
        R[...] = total.astype(BF16)

        @pl.when(r == 0)
        def _():
            mine = pltpu.make_async_copy(R.at[tokens(y * tok)], Q.at[zl], loc.at[3])
            mine.start()
            mine.wait()

        @pl.when(r != 0)
        def _():
            q_copy(0).start()

        for t in (1, 2, 3):
            q_copy(t).start()

    def out_spread():
        for t in (0, 1, 2, 3):
            j = (zl + t) % 4

            def wait(j=j):
                arrived(Q.at[j], qs.at[0], qr.at[j], core)

            if t == 0:
                pl.when(r != 0)(wait)
            else:
                wait()
        for dx in (1, 2, 3):
            o_copy(dx).start()
        O[x] = Q[x]

    def out_done():
        for dx in (1, 2, 3):
            g = (x + dx) % 4
            arrived(O.at[g], ors.at[0], orr.at[g], core)
        for g in range(4):
            ig_out[:, g * quarter : (g + 1) * quarter] = O[g]

    p_jobs = (
        bound_for(0, 0),
        jnp.where(r == 0, h, bound_for(1, 0)),
        bound_for(0, 1),
        bound_for(1, 1),
    )
    t_jobs = (
        held_from(0, 0),
        jnp.where(r == 0, held_from(0, 1), held_from(1, 0)),
        jnp.where(r == 0, held_from(1, 1), held_from(0, 1)),
        jnp.where(r == 0, held_from(0, 2), held_from(1, 1)),
    )
    late = 2 * NC + 4 * HOP

    def pick(s, pairs, jobs):
        g = jobs[0]
        for at, job in zip(pairs[1:], jobs[1:], strict=True):
            g = jnp.where(s == at, job, g)
        return g

    p_at = (START, START + 1, START + 3, START + 4)
    t_at = (START + 6, START + 8, late - 1, late + 1)

    def step(s, _):
        for d in (0, 1):
            w_step(d, s)
        for at, job in ((1, in_places), (4, in_spread), (5, grad_relay), (8, in_cores), (START, in_done)):
            pl.when(s == at)(job)

        @pl.when(functools.reduce(jnp.logical_or, [s == at for at in p_at]))
        def _():
            p_job(pick(s, p_at, p_jobs))

        for d in (0, 1):
            d_step(d, s - START - 2)
        last_step(s - START - 2)

        @pl.when(functools.reduce(jnp.logical_or, [s == at for at in t_at]))
        def _():
            t_job(pick(s, t_at, t_jobs))

        for at, job in ((late + 2, x_send), (late + 6, x_sum), (late + 9, out_spread)):
            pl.when(s == at)(job)
        return 0

    lax.fori_loop(0, START + 2 + 2 * NC + 6 * HOP, step, 0)
    out_done()

    def leave(i, _):
        for d in (0, 1):
            w_copy(d, 0, i).wait_send()
            d_copy(d, 1, i).wait_send()

            @pl.when((rd[d] != 3) | in_half(d, i))
            def _(d=d):
                w_copy(d, 1, i).wait_send()

            @pl.when((rd[d] != 0) | in_half(d, i))
            def _(d=d):
                d_copy(d, 0, i).wait_send()

            @pl.when((r == 0) | ((rd[1] == 1 + 2 * d) & (i % 2 == d)))
            def _(d=d):
                y_copy(d, i).wait_send()

        return 0

    lax.fori_loop(0, NC, leave, 0)
    for d in (0, 1):
        for k in (0, 1):
            g_copy(d, k).wait_send()
        g2_copy(d).wait_send()
    for n in (1, 2, 3):
        for copy in (s1_copy, s2_copy, s3_copy, xr_copy, q_copy, o_copy):
            copy(n).wait_send()

    @pl.when(r != 0)
    def _():
        s2_copy(0).wait_send()
        q_copy(0).wait_send()

    for g in range(4):
        s4_copy(g).wait_send()
        ct_copy(g).wait_send()


def per_device(inputs, out_grad, weight):
    tok, width = inputs.shape
    rows, hidden = weight.shape
    quarter = width // 4
    sems = pltpu.SemaphoreType.DMA
    vmem = pl.BlockSpec(memory_space=pltpu.VMEM)
    return pl.pallas_call(
        kernel,
        out_shape=(
            jax.ShapeDtypeStruct((tok, width), BF16),
            jax.ShapeDtypeStruct((rows, hidden), BF16),
        ),
        in_specs=[vmem] * 3,
        out_specs=(vmem, vmem),
        scratch_shapes=[
            pltpu.VMEM((8 * tok, hidden), BF16),
            pltpu.VMEM((4, rows, hidden), BF16),
            pltpu.VMEM((4, 8 * tok, quarter), BF16),
            pltpu.VMEM((4, tok, quarter), BF16),
            pltpu.VMEM((4, rows, hidden), F32),
            pltpu.VMEM((2, 3, rows, hidden), BF16),
            pltpu.VMEM((4, 8 * tok, quarter), BF16),
            pltpu.VMEM((4, 4 * tok, quarter), BF16),
            pltpu.VMEM((4, 4 * tok, quarter), BF16),
            pltpu.VMEM((4, 4 * tok, quarter), BF16),
            pltpu.VMEM((4 * tok, quarter), BF16),
            pltpu.VMEM((4, tok, quarter), BF16),
            pltpu.VMEM((4, tok, quarter), BF16),
            pltpu.VMEM((rows, hidden), BF16),
            sems((2, 2, NC)), sems((2, 2, NC)), sems((2, 2, NC)), sems((2, 2, NC)),
            sems((NC,)), sems((2, NC)),
            sems((2, 2)), sems((2, 2)), sems((2,)), sems((2,)),
            *[sems((4,)) for _ in range(16)],
            sems((4,)),
        ],
        compiler_params=pltpu.CompilerParams(
            collective_id=0, has_side_effects=True, vmem_limit_bytes=56 * 2**20
        ),
        cost_estimate=pl.CostEstimate(
            flops=4 * 8 * tok * width * hidden, bytes_accessed=4 * 2**20, transcendentals=0
        ),
        name="backward",
    )(inputs, out_grad, weight)


def solution(mesh):
    return jax.shard_map(
        per_device,
        mesh=mesh,
        in_specs=(P(("dp", "gx", "gz"), "gy"), P(("dp", "gx", "gy"), "gz"), P(("gy", "gx"), "gz")),
        out_specs=(P(("dp", "gx", "gz"), "gy"), P(("gy", "gx"), "gz")),
        check_vma=False,
    )
```

time: 520 us -> 151 us (0.29)
  the two profiles are of different devices: /device:TPU:8 before, /device:TPU:22 now
where the time goes in v2:
time: 151 us
  Pallas kernels  147 us (97%)
  local copies, waits for them, and re-layouts  3.78 us (3%)
    pallas_call x1, Pallas kernels, per_device(): pl.pallas_call(kernel, out_shape=(jax.ShapeDtypeStruct((tok, width), BF16...  147 us
    unnamed x2, local copies, waits for them, and re-layouts  3.78 us

profile of v2, /device:TPU:22, one launch (start us, length us, event | category | flops | bytes accessed | tf_op | source)
XLA Modules:
  0.0 151.2 jit_solution(18302165938343236566)
XLA Ops:
  0.6 146.8 %backward.1 = (bf16[96,1024]{1,0:T(8,128)(2,1)}, bf16[256,1792]{1,0:T(8,128)(2,1)}) custom-call(bf16[96,1024]{1,0:T(8,128)(2,1)} %inp.1, bf16[192,1792]{1,0:T(8,128)(2,1)} %og.1, bf16[256,1792]{1,0:T(8,128)(2,1)} %wt.1), custom_call_target="tpu_custom_call" | custom-call | flops 5637144576 | bytes 4194304 | tf_op jit(solution)/shard_map/backward/pallas_call | solution.py:481
  147.4 1.6 %copy.7 = bf16[96,1024]{1,0:T(8,128)(2,1)} copy(bf16[96,1024]{1,0:T(8,128)(2,1)} %get-tuple-element.4) | data formatting | bytes 393216
  149.0 2.2 %copy.8 = bf16[256,1792]{1,0:T(8,128)(2,1)} copy(bf16[256,1792]{1,0:T(8,128)(2,1)} %get-tuple-element.5) | data formatting | bytes 1835008

commit v3 on v2

--- a/solution.py
+++ b/solution.py
@@ -9,16 +9,18 @@
 
 MESH = pl.DeviceIdType.MESH
 NC = 8
+UNIT = NC // 8
+AHEAD = 1
 HOP = 2
 START = 12
 BF16, F32 = jnp.bfloat16, jnp.float32
 
 
 def kernel(
-    inp, og, wt, ig_out, wg_out,
-    G, W, X, I1, PT, RD, T, CT, S, XR, R, Q, O, FB,
-    wr, ws, dr, dss, yr, ysd, gr, gs, g2r, g2s, s1r, s1s, s2r, s2s, s3r, s3s, s4r, s4s,
-    ctr, cts, xrr, xrs, qr, qs, orr, ors, loc,
+    inp, og, wt, O, wg_out,
+    G, W, X, I1, I2, PT, RD, T, CT, S, XR, R, Q1, Q, FB,
+    wr, ws, dr, dss, yr, ysd, gr, gs, g2r, g2s, s1r, s1s, s2r, s2s, s3r, s3s, s4r, s4s, s5r, s5s,
+    ctr, cts, xrr, xrs, qr, qs, q1r, q1s, orr, ors, loc,
 ):
     y, h, zl = lax.axis_index("dp"), lax.axis_index("gx"), lax.axis_index("gy")
     gz = lax.axis_index("gz")
@@ -93,8 +95,12 @@
         return remote(inp.at[:, columns(to)], I1.at[x], s1s.at[dx], s1r.at[x], xdev(to))
 
     def s2_copy(t):
-        j = (zl + t) % 4
-        return remote(I1.at[j], X.at[x, tokens(c * half + y * tok)], s2s.at[t], s2r.at[y], {"dp": zl, "gy": j})
+        to = (zl + t) % 4
+        return remote(I1.at[to], I2.at[zl], s2s.at[t], s2r.at[zl], {"gy": to})
+
+    def s5_copy(t):
+        to = (y + t) % 4
+        return remote(I2.at[to], X.at[x, tokens(c * half + y * tok)], s5s.at[t], s5r.at[y], {"dp": to})
 
     def s3_copy(dx):
         part = X.at[x, halves(c)]
@@ -111,9 +117,13 @@
         to = (x + dx) % 4
         return remote(S.at[to], XR.at[x], xrs.at[dx], xrr.at[x], xdev(to))
 
+    def q1_copy(t):
+        to = (y + t) % 4
+        return remote(R.at[tokens(to * tok)], Q1.at[y], q1s.at[t], q1r.at[y], {"dp": to})
+
     def q_copy(t):
-        k = (y + t) % 4
-        return remote(R.at[tokens(k * tok)], Q.at[zl], qs.at[t], qr.at[zl], {"dp": k, "gy": y})
+        to = (zl + t) % 4
+        return remote(Q1.at[to], Q.at[zl], qs.at[t], qr.at[zl], {"gy": to})
 
     def o_copy(dx):
         to = (x + dx) % 4
@@ -127,19 +137,12 @@
     def greet(dev):
         pl.semaphore_signal(barrier, inc=1, device_id=dev, device_id_type=MESH)
 
-    for dev in (*right, *ydev, core):
+    for dev in (*right, core):
         greet(dev)
-    for dx in (1, 2, 3):
-        greet(xdev((x + dx) % 4))
     for t in (1, 2, 3):
-        greet({"dp": zl, "gy": (zl + t) % 4})
-        greet({"dp": (y + t) % 4, "gy": y})
-
-    @pl.when(r != 0)
-    def _():
-        greet({"dp": zl, "gy": zl})
-        greet({"dp": y, "gy": y})
-
+        greet(xdev((x + t) % 4))
+        greet({"dp": (y + t) % 4})
+        greet({"gy": (zl + t) % 4})
     own = [
         pltpu.make_async_copy(og.at[pl.ds(k * tok, tok)], G.at[tokens(k * half + y * tok)], loc.at[k]) for k in (0, 1)
     ]
@@ -155,22 +158,20 @@
 
     for copy in own:
         copy.wait()
-    pl.semaphore_wait(barrier, jnp.where(r == 0, 14, 16))
-
+    pl.semaphore_wait(barrier, 12)
     for dx in (1, 2, 3):
         s1_copy(dx).start()
-    for k in (0, 1):
-        g_copy(0, k).start()
-        g_copy(1, 1 - k).start()
-
-    @pl.when(r == 0)
-    def _():
-        def first(i, _):
+    for d in (0, 1):
+        g_copy(d, d).start()
+
+    def w_own(i):
+        @pl.when((r == 0) & (i < NC))
+        def _():
             w_copy(0, 0, i).start()
             w_copy(1, 0, i).start()
-            return 0
-
-        lax.fori_loop(0, NC, first, 0)
+
+    for i in range(AHEAD):
+        w_own(i)
 
     def w_step(d, s):
         m = s - HOP * rr[d]
@@ -233,7 +234,6 @@
             total = PT[h, chunk(i), :] + RD[0, 2, chunk(i), :].astype(F32) + RD[1, 2, chunk(i), :].astype(F32)
             mean = (total / groups).astype(BF16)
             FB[chunk(i), :] = mean
-            wg_out[chunk(i), :] = mean
             y_copy(0, i).start()
             y_copy(1, i).start()
 
@@ -252,25 +252,24 @@
             def _():
                 y_copy(1, n).start()
 
-            wg_out[chunk(n), :] = FB[chunk(n), :]
-
     def in_places():
         for dx in (1, 2, 3):
             j = (x + dx) % 4
             arrived(I1.at[j], s1s.at[0], s1r.at[j], core)
 
-        @pl.when(r == 0)
-        def _():
-            mine = pltpu.make_async_copy(I1.at[zl], X.at[x, tokens(c * half + y * tok)], loc.at[3])
-            mine.start()
-            mine.wait()
-
-        @pl.when(r != 0)
-        def _():
-            s2_copy(0).start()
-
         for t in (1, 2, 3):
             s2_copy(t).start()
+        I2[zl] = I1[zl]
+
+    def in_columns():
+        for t in (1, 2, 3):
+            j = (zl + t) % 4
+            arrived(I2.at[j], s2s.at[0], s2r.at[j], core)
+        for t in (1, 2, 3):
+            s5_copy(t).start()
+        for d in (0, 1):
+            g_copy(d, 1 - d).start()
+        X[x, tokens(c * half + y * tok), :] = I2[y]
 
     def grad_relay():
         for d in (0, 1):
@@ -279,16 +278,9 @@
             g2_copy(d).start()
 
     def in_spread():
-        for t in (0, 1, 2, 3):
+        for t in (1, 2, 3):
             k = (y + t) % 4
-
-            def wait(k=k):
-                arrived(X.at[x, tokens(c * half + k * tok)], s2s.at[0], s2r.at[k], core)
-
-            if t == 0:
-                pl.when(r != 0)(wait)
-            else:
-                wait()
+            arrived(X.at[x, tokens(c * half + k * tok)], s5s.at[0], s5r.at[k], core)
         for dx in (1, 2, 3):
             s3_copy(dx).start()
         s4_copy(x).start()
@@ -318,20 +310,15 @@
 
         lax.fori_loop(0, G.shape[1] // 256, tile, 0)
 
-    def t_job(g):
-        def part(n, _):
-            where = halves((1 - c + n) % 2)
-            T[g, where, :] = lax.dot_general(
-                G[where, :], W[g], (((1,), (1,)), ((), ())), preferred_element_type=F32
-            ).astype(BF16)
-
-            @pl.when(n == 0)
-            def _():
-                ct_copy(g).start()
-
-            return 0
-
-        lax.fori_loop(0, 2, part, 0)
+    def t_job(g, n):
+        where = halves((1 - c + n) % 2)
+        T[g, where, :] = lax.dot_general(
+            G[where, :], W[g], (((1,), (1,)), ((), ())), preferred_element_type=F32
+        ).astype(BF16)
+
+        @pl.when(n == 0)
+        def _():
+            ct_copy(g).start()
 
     def cores_sum(g):
         arrived(CT.at[g], cts.at[0], ctr.at[g], core)
@@ -351,40 +338,34 @@
             total = total + XR[g].astype(F32)
         R[...] = total.astype(BF16)
 
-        @pl.when(r == 0)
-        def _():
-            mine = pltpu.make_async_copy(R.at[tokens(y * tok)], Q.at[zl], loc.at[3])
-            mine.start()
-            mine.wait()
-
-        @pl.when(r != 0)
-        def _():
-            q_copy(0).start()
-
+        for t in (1, 2, 3):
+            q1_copy(t).start()
+        Q1[y] = R[tokens(y * tok), :]
+
+    def out_planes():
+        for t in (1, 2, 3):
+            f = (y + t) % 4
+            arrived(Q1.at[f], q1s.at[0], q1r.at[f], core)
         for t in (1, 2, 3):
             q_copy(t).start()
+        Q[zl] = Q1[zl]
 
     def out_spread():
-        for t in (0, 1, 2, 3):
+        for t in (1, 2, 3):
             j = (zl + t) % 4
-
-            def wait(j=j):
-                arrived(Q.at[j], qs.at[0], qr.at[j], core)
-
-            if t == 0:
-                pl.when(r != 0)(wait)
-            else:
-                wait()
+            arrived(Q.at[j], qs.at[0], qr.at[j], core)
         for dx in (1, 2, 3):
             o_copy(dx).start()
-        O[x] = Q[x]
+        pltpu.make_async_copy(Q.at[x], O.at[x], loc.at[0]).start()
 
     def out_done():
+        pltpu.make_async_copy(FB, wg_out, loc.at[1]).start()
         for dx in (1, 2, 3):
             g = (x + dx) % 4
             arrived(O.at[g], ors.at[0], orr.at[g], core)
-        for g in range(4):
-            ig_out[:, g * quarter : (g + 1) * quarter] = O[g]
+        pltpu.make_async_copy(Q.at[x], O.at[x], loc.at[0]).wait()
+        pltpu.make_async_copy(FB, wg_out, loc.at[1]).wait()
+
 
     p_jobs = (
         bound_for(0, 0),
@@ -406,13 +387,17 @@
             g = jnp.where(s == at, job, g)
         return g
 
-    p_at = (START, START + 1, START + 3, START + 4)
-    t_at = (START + 6, START + 8, late - 1, late + 1)
+    p_at = (START, START + 1, START + 2 + UNIT, START + 2 + 2 * UNIT)
+    t_at = (*(START + 3 * UNIT + k for k in range(4)), *(late - 1 + k for k in range(4)))
 
     def step(s, _):
+        w_own(s + AHEAD)
         for d in (0, 1):
             w_step(d, s)
-        for at, job in ((1, in_places), (4, in_spread), (5, grad_relay), (8, in_cores), (START, in_done)):
+        for at, job in (
+            (UNIT, in_places), (3 * UNIT, in_columns), (4 * UNIT, grad_relay),
+            (5 * UNIT, in_spread), (9 * UNIT, in_cores), (START, in_done),
+        ):
             pl.when(s == at)(job)
 
         @pl.when(functools.reduce(jnp.logical_or, [s == at for at in p_at]))
@@ -425,9 +410,13 @@
 
         @pl.when(functools.reduce(jnp.logical_or, [s == at for at in t_at]))
         def _():
-            t_job(pick(s, t_at, t_jobs))
-
-        for at, job in ((late + 2, x_send), (late + 6, x_sum), (late + 9, out_spread)):
+            n = functools.reduce(jnp.logical_or, [s == at for at in t_at[1::2]]).astype(jnp.int32)
+            t_job(pick(s, t_at, [g for g in t_jobs for _ in (0, 1)]), n)
+
+        for at, job in (
+            (late + 3, x_send), (late + 3 + 3 * UNIT, x_sum), (late + 3 + 5 * UNIT, out_planes),
+            (late + 3 + 7 * UNIT, out_spread),
+        ):
             pl.when(s == at)(job)
         return 0
 
@@ -447,9 +436,18 @@
             def _(d=d):
                 d_copy(d, 0, i).wait_send()
 
-            @pl.when((r == 0) | ((rd[1] == 1 + 2 * d) & (i % 2 == d)))
-            def _(d=d):
-                y_copy(d, i).wait_send()
+        @pl.when(r == 0)
+        def _():
+            y_copy(0, i).wait_send()
+            y_copy(1, i).wait_send()
+
+        @pl.when((rd[1] == 1) & (i % 2 == 0))
+        def _():
+            y_copy(0, i).wait_send()
+
+        @pl.when((rd[1] == 3) & (i % 2 == 1))
+        def _():
+            y_copy(1, i).wait_send()
 
         return 0
 
@@ -459,17 +457,19 @@
             g_copy(d, k).wait_send()
         g2_copy(d).wait_send()
     for n in (1, 2, 3):
-        for copy in (s1_copy, s2_copy, s3_copy, xr_copy, q_copy, o_copy):
+        for copy in (s1_copy, s2_copy, s5_copy, s3_copy, xr_copy, q1_copy, q_copy, o_copy):
             copy(n).wait_send()
-
-    @pl.when(r != 0)
-    def _():
-        s2_copy(0).wait_send()
-        q_copy(0).wait_send()
 
     for g in range(4):
         s4_copy(g).wait_send()
         ct_copy(g).wait_send()
+
+
+def place(parts, shard, ig_out, wg_out):
+    count, _, quarter = parts.shape
+    for g in range(count):
+        ig_out[:, g * quarter : (g + 1) * quarter] = parts[g]
+    wg_out[...] = shard[...]
 
 
 def per_device(inputs, out_grad, weight):
@@ -478,18 +478,20 @@
     quarter = width // 4
     sems = pltpu.SemaphoreType.DMA
     vmem = pl.BlockSpec(memory_space=pltpu.VMEM)
-    return pl.pallas_call(
+    hbm = pl.BlockSpec(memory_space=pl.ANY)
+    parts, weight_grad = pl.pallas_call(
         kernel,
         out_shape=(
-            jax.ShapeDtypeStruct((tok, width), BF16),
+            jax.ShapeDtypeStruct((4, tok, quarter), BF16),
             jax.ShapeDtypeStruct((rows, hidden), BF16),
         ),
-        in_specs=[vmem] * 3,
-        out_specs=(vmem, vmem),
+        in_specs=[hbm] * 3,
+        out_specs=(hbm, hbm),
         scratch_shapes=[
             pltpu.VMEM((8 * tok, hidden), BF16),
             pltpu.VMEM((4, rows, hidden), BF16),
             pltpu.VMEM((4, 8 * tok, quarter), BF16),
+            pltpu.VMEM((4, tok, quarter), BF16),
             pltpu.VMEM((4, tok, quarter), BF16),
             pltpu.VMEM((4, rows, hidden), F32),
             pltpu.VMEM((2, 3, rows, hidden), BF16),
@@ -504,7 +506,7 @@
             sems((2, 2, NC)), sems((2, 2, NC)), sems((2, 2, NC)), sems((2, 2, NC)),
             sems((NC,)), sems((2, NC)),
             sems((2, 2)), sems((2, 2)), sems((2,)), sems((2,)),
-            *[sems((4,)) for _ in range(16)],
+            *[sems((4,)) for _ in range(20)],
             sems((4,)),
         ],
         compiler_params=pltpu.CompilerParams(
@@ -515,6 +517,16 @@
         ),
         name="backward",
     )(inputs, out_grad, weight)
+    return pl.pallas_call(
+        place,
+        out_shape=(
+            jax.ShapeDtypeStruct((tok, width), BF16),
+            jax.ShapeDtypeStruct((rows, hidden), BF16),
+        ),
+        in_specs=[vmem] * 2,
+        out_specs=(vmem, vmem),
+        name="place",
+    )(parts, weight_grad)
 
 
 def solution(mesh):

time: 151 us -> 130 us (0.86)
  the two profiles are of different devices: /device:TPU:22 before, /device:TPU:58 now
where the time goes in v3:
time: 130 us
  Pallas kernels  129 us (99%)
    pallas_call x1, Pallas kernels, per_device(): pl.pallas_call(kernel, out_shape=(jax.ShapeDtypeStruct((4, tok, quarter),...  127 us

profile of v3, /device:TPU:58, one launch (start us, length us, event | category | flops | bytes accessed | tf_op | source)
XLA Modules:
  0.0 129.8 jit_solution(15619625409583993748)
XLA Ops:
  0.6 126.9 %backward.1 = (bf16[4,96,256]{2,1,0:T(8,128)(2,1)}, bf16[256,1792]{1,0:T(8,128)(2,1)}) custom-call(bf16[96,1024]{1,0:T(8,128)(2,1)} %inp.1, bf16[192,1792]{1,0:T(8,128)(2,1)} %og.1, bf16[256,1792]{1,0:T(8,128)(2,1)} %wt.1), custom_call_target="tpu_custom_call" | custom-call | flops 5637144576 | bytes 4194304 | tf_op jit(solution)/shard_map/backward/pallas_call | solution.py:482
  127.5 2.3 %place.1 = (bf16[96,1024]{1,0:T(8,128)(2,1)}, bf16[256,1792]{1,0:T(8,128)(2,1)}) custom-call(bf16[4,96,256]{2,1,0:T(8,128)(2,1)} %get-tuple-element.4.parts, bf16[256,1792]{1,0:T(8,128)(2,1)} %get-tuple-element.5.shard), custom_call_target="tpu_custom_call" | custom-call | tf_op jit(solution)/shard_map/place/pallas_call | solution.py:520

commit v4 on v3

--- a/solution.py
+++ b/solution.py
@@ -11,6 +11,7 @@
 NC = 8
 UNIT = NC // 8
 AHEAD = 1
+LEAD = 2
 HOP = 2
 START = 12
 BF16, F32 = jnp.bfloat16, jnp.float32
@@ -19,7 +20,7 @@
 def kernel(
     inp, og, wt, O, wg_out,
     G, W, X, I1, I2, PT, RD, T, CT, S, XR, R, Q1, Q, FB,
-    wr, ws, dr, dss, yr, ysd, gr, gs, g2r, g2s, s1r, s1s, s2r, s2s, s3r, s3s, s4r, s4s, s5r, s5s,
+    wr, ws, dr, dss, yr, ysd, y2r, y2s, kept, gr, gs, g2r, g2s, s1r, s1s, s2r, s2s, s3r, s3s, s4r, s4s, s5r, s5s,
     ctr, cts, xrr, xrs, qr, qs, q1r, q1s, orr, ors, loc,
 ):
     y, h, zl = lax.axis_index("dp"), lax.axis_index("gx"), lax.axis_index("gy")
@@ -68,6 +69,9 @@
     def chunk(i):
         return pl.ds(pl.multiple_of(i * rows, rows), rows)
 
+    def chunk_half(i, d):
+        return pl.ds(pl.multiple_of(i * rows + d * (rows // 2), rows // 2), rows // 2)
+
     def columns(q):
         return pl.ds(pl.multiple_of(q * quarter, 128), quarter)
 
@@ -81,6 +85,13 @@
 
     def y_copy(d, i):
         return remote(FB.at[chunk(i)], FB.at[chunk(i)], ysd.at[d, i], yr.at[i], ydev[d])
+
+    def y2_copy(d, i):
+        part = FB.at[chunk_half(i, d)]
+        return remote(part, part, y2s.at[d, i], y2r.at[d, i], ydev[d])
+
+    def stored(i):
+        return pltpu.make_async_copy(FB.at[chunk(i)], wg_out.at[chunk(i)], kept.at[i])
 
     def g_copy(d, k):
         part = G.at[tokens(k * half + y * tok)]
@@ -156,11 +167,11 @@
         held.start()
         held.wait()
 
-    for copy in own:
-        copy.wait()
     pl.semaphore_wait(barrier, 12)
     for dx in (1, 2, 3):
         s1_copy(dx).start()
+    for copy in own:
+        copy.wait()
     for d in (0, 1):
         g_copy(d, d).start()
 
@@ -236,21 +247,31 @@
             FB[chunk(i), :] = mean
             y_copy(0, i).start()
             y_copy(1, i).start()
+            stored(i).start()
 
         away = rd[1]
         n = i - HOP * jnp.where(away == 2, 2, 1)
 
         @pl.when((r != 0) & (n >= 0) & (n < NC))
         def _():
-            arrived(FB.at[chunk(n)], ysd.at[0, 0], yr.at[n], ydev[0])
-
-            @pl.when((away == 1) & (n % 2 == 0))
-            def _():
-                y_copy(0, n).start()
-
-            @pl.when((away == 3) & (n % 2 == 1))
-            def _():
-                y_copy(1, n).start()
+            @pl.when(away != 2)
+            def _():
+                arrived(FB.at[chunk(n)], ysd.at[0, 0], yr.at[n], ydev[0])
+
+            @pl.when(away == 1)
+            def _():
+                y2_copy(0, n).start()
+
+            @pl.when(away == 3)
+            def _():
+                y2_copy(1, n).start()
+
+            @pl.when(away == 2)
+            def _():
+                for d in (0, 1):
+                    arrived(FB.at[chunk_half(n, d)], y2s.at[0, 0], y2r.at[d, n], ydev[0])
+
+            stored(n).start()
 
     def in_places():
         for dx in (1, 2, 3):
@@ -359,13 +380,10 @@
         pltpu.make_async_copy(Q.at[x], O.at[x], loc.at[0]).start()
 
     def out_done():
-        pltpu.make_async_copy(FB, wg_out, loc.at[1]).start()
         for dx in (1, 2, 3):
             g = (x + dx) % 4
             arrived(O.at[g], ors.at[0], orr.at[g], core)
         pltpu.make_async_copy(Q.at[x], O.at[x], loc.at[0]).wait()
-        pltpu.make_async_copy(FB, wg_out, loc.at[1]).wait()
-
 
     p_jobs = (
         bound_for(0, 0),
@@ -405,8 +423,8 @@
             p_job(pick(s, p_at, p_jobs))
 
         for d in (0, 1):
-            d_step(d, s - START - 2)
-        last_step(s - START - 2)
+            d_step(d, s - START - LEAD)
+        last_step(s - START - LEAD)
 
         @pl.when(functools.reduce(jnp.logical_or, [s == at for at in t_at]))
         def _():
@@ -420,7 +438,7 @@
             pl.when(s == at)(job)
         return 0
 
-    lax.fori_loop(0, START + 2 + 2 * NC + 6 * HOP, step, 0)
+    lax.fori_loop(0, START + LEAD + 2 * NC + 6 * HOP, step, 0)
     out_done()
 
     def leave(i, _):
@@ -441,14 +459,15 @@
             y_copy(0, i).wait_send()
             y_copy(1, i).wait_send()
 
-        @pl.when((rd[1] == 1) & (i % 2 == 0))
-        def _():
-            y_copy(0, i).wait_send()
-
-        @pl.when((rd[1] == 3) & (i % 2 == 1))
-        def _():
-            y_copy(1, i).wait_send()
-
+        @pl.when(rd[1] == 1)
+        def _():
+            y2_copy(0, i).wait_send()
+
+        @pl.when(rd[1] == 3)
+        def _():
+            y2_copy(1, i).wait_send()
+
+        stored(i).wait()
         return 0
 
     lax.fori_loop(0, NC, leave, 0)
@@ -465,11 +484,25 @@
         ct_copy(g).wait_send()
 
 
-def place(parts, shard, ig_out, wg_out):
+def place(parts, shard, ig_out, wg_out, ig_held, wg_held, sem_in, sem_out):
     count, _, quarter = parts.shape
+    rows = shard.shape[0] // count
+    pairs = []
     for g in range(count):
-        ig_out[:, g * quarter : (g + 1) * quarter] = parts[g]
-    wg_out[...] = shard[...]
+        block = pl.ds(g * rows, rows)
+        pairs.append((shard.at[block], wg_held.at[block], wg_out.at[block]))
+    for g in range(count):
+        columns = pl.ds(g * quarter, quarter)
+        pairs.append((parts.at[g], ig_held.at[:, columns], ig_out.at[:, columns]))
+    loads = [pltpu.make_async_copy(a, b, sem_in.at[n]) for n, (a, b, _) in enumerate(pairs)]
+    stores = [pltpu.make_async_copy(b, c, sem_out.at[n]) for n, (_, b, c) in enumerate(pairs)]
+    for load in loads:
+        load.start()
+    for load, store in zip(loads, stores, strict=True):
+        load.wait()
+        store.start()
+    for store in stores:
+        store.wait()
 
 
 def per_device(inputs, out_grad, weight):
@@ -477,7 +510,6 @@
     rows, hidden = weight.shape
     quarter = width // 4
     sems = pltpu.SemaphoreType.DMA
-    vmem = pl.BlockSpec(memory_space=pltpu.VMEM)
     hbm = pl.BlockSpec(memory_space=pl.ANY)
     parts, weight_grad = pl.pallas_call(
         kernel,
@@ -504,7 +536,7 @@
             pltpu.VMEM((4, tok, quarter), BF16),
             pltpu.VMEM((rows, hidden), BF16),
             sems((2, 2, NC)), sems((2, 2, NC)), sems((2, 2, NC)), sems((2, 2, NC)),
-            sems((NC,)), sems((2, NC)),
+            sems((NC,)), sems((2, NC)), sems((2, NC)), sems((2, NC)), sems((NC,)),
             sems((2, 2)), sems((2, 2)), sems((2,)), sems((2,)),
             *[sems((4,)) for _ in range(20)],
             sems((4,)),
@@ -523,8 +555,11 @@
             jax.ShapeDtypeStruct((tok, width), BF16),
             jax.ShapeDtypeStruct((rows, hidden), BF16),
         ),
-        in_specs=[vmem] * 2,
-        out_specs=(vmem, vmem),
+        in_specs=[hbm] * 2,
+        out_specs=(hbm, hbm),
+        scratch_shapes=[
+            pltpu.VMEM((tok, width), BF16), pltpu.VMEM((rows, hidden), BF16), sems((8,)), sems((8,)),
+        ],
         name="place",
     )(parts, weight_grad)
 

time: 130 us -> 129 us (level)
  no operation moved by 1% of the time
where the time goes in v4:
time: 129 us
  Pallas kernels  128 us (99%)
    pallas_call x1, Pallas kernels, per_device(): pl.pallas_call(kernel, out_shape=(jax.ShapeDtypeStruct((4, tok, quarter),...  126 us

profile of v4, /device:TPU:58, one launch (start us, length us, event | category | flops | bytes accessed | tf_op | source)
XLA Modules:
  0.0 128.9 jit_solution(16362772416166175636)
XLA Ops:
  0.6 126.1 %backward.1 = (bf16[4,96,256]{2,1,0:T(8,128)(2,1)}, bf16[256,1792]{1,0:T(8,128)(2,1)}) custom-call(bf16[96,1024]{1,0:T(8,128)(2,1)} %inp.1, bf16[192,1792]{1,0:T(8,128)(2,1)} %og.1, bf16[256,1792]{1,0:T(8,128)(2,1)} %wt.1), custom_call_target="tpu_custom_call" | custom-call | flops 5637144576 | bytes 4194304 | tf_op jit(solution)/shard_map/backward/pallas_call | solution.py:514
  126.7 2.2 %place.1 = (bf16[96,1024]{1,0:T(8,128)(2,1)}, bf16[256,1792]{1,0:T(8,128)(2,1)}) custom-call(bf16[4,96,256]{2,1,0:T(8,128)(2,1)} %get-tuple-element.4.parts, bf16[256,1792]{1,0:T(8,128)(2,1)} %get-tuple-element.5.shard), custom_call_target="tpu_custom_call" | custom-call | tf_op jit(solution)/shard_map/place/pallas_call | solution.py:552

commit v5 on v4

--- a/solution.py
+++ b/solution.py
@@ -413,8 +413,8 @@
         for d in (0, 1):
             w_step(d, s)
         for at, job in (
-            (UNIT, in_places), (3 * UNIT, in_columns), (4 * UNIT, grad_relay),
-            (5 * UNIT, in_spread), (9 * UNIT, in_cores), (START, in_done),
+            (0, in_places), (2 * UNIT, in_columns), (4 * UNIT, grad_relay),
+            (5 * UNIT, in_spread), (8 * UNIT, in_cores), (START, in_done),
         ):
             pl.when(s == at)(job)
 
@@ -432,8 +432,8 @@
             t_job(pick(s, t_at, [g for g in t_jobs for _ in (0, 1)]), n)
 
         for at, job in (
-            (late + 3, x_send), (late + 3 + 3 * UNIT, x_sum), (late + 3 + 5 * UNIT, out_planes),
-            (late + 3 + 7 * UNIT, out_spread),
+            (late + 3, x_send), (late + 3 + 4 * UNIT, x_sum), (late + 3 + 7 * UNIT, out_planes),
+            (late + 3 + 10 * UNIT, out_spread),
         ):
             pl.when(s == at)(job)
         return 0

time: 129 us -> 128 us (level)
  the two profiles are of different devices: /device:TPU:58 before, /device:TPU:64 now
where the time goes in v5:
time: 128 us
  Pallas kernels  127 us (99%)
    pallas_call x1, Pallas kernels, per_device(): pl.pallas_call(kernel, out_shape=(jax.ShapeDtypeStruct((4, tok, quarter),...  125 us

profile of v5, /device:TPU:64, one launch (start us, length us, event | category | flops | bytes accessed | tf_op | source)
XLA Modules:
  0.0 127.6 jit_solution(13332214107343580157)
XLA Ops:
  0.6 124.8 %backward.1 = (bf16[4,96,256]{2,1,0:T(8,128)(2,1)}, bf16[256,1792]{1,0:T(8,128)(2,1)}) custom-call(bf16[96,1024]{1,0:T(8,128)(2,1)} %inp.1, bf16[192,1792]{1,0:T(8,128)(2,1)} %og.1, bf16[256,1792]{1,0:T(8,128)(2,1)} %wt.1), custom_call_target="tpu_custom_call" | custom-call | flops 5637144576 | bytes 4194304 | tf_op jit(solution)/shard_map/backward/pallas_call | solution.py:514
  125.4 2.2 %place.1 = (bf16[96,1024]{1,0:T(8,128)(2,1)}, bf16[256,1792]{1,0:T(8,128)(2,1)}) custom-call(bf16[4,96,256]{2,1,0:T(8,128)(2,1)} %get-tuple-element.4.parts, bf16[256,1792]{1,0:T(8,128)(2,1)} %get-tuple-element.5.shard), custom_call_target="tpu_custom_call" | custom-call | tf_op jit(solution)/shard_map/place/pallas_call | solution.py:552

commit v6 on v5

--- a/solution.py
+++ b/solution.py
@@ -345,11 +345,12 @@
         arrived(CT.at[g], cts.at[0], ctr.at[g], core)
         S[g] = (T[g, halves(c), :].astype(F32) + CT[g].astype(F32)).astype(BF16)
 
-    def x_send():
-        for g in range(4):
-            cores_sum(g)
-        for dx in (1, 2, 3):
-            xr_copy(dx).start()
+    def x_send(g):
+        cores_sum(g)
+
+        @pl.when(g != x)
+        def _():
+            xr_copy((g - x + 4) % 4).start()
 
     def x_sum():
         total = S[x].astype(F32)
@@ -407,6 +408,7 @@
 
     p_at = (START, START + 1, START + 2 + UNIT, START + 2 + 2 * UNIT)
     t_at = (*(START + 3 * UNIT + k for k in range(4)), *(late - 1 + k for k in range(4)))
+    x_at = (START + 8 * UNIT, START + 9 * UNIT, late + 2, late + 4)
 
     def step(s, _):
         w_own(s + AHEAD)
@@ -431,8 +433,12 @@
             n = functools.reduce(jnp.logical_or, [s == at for at in t_at[1::2]]).astype(jnp.int32)
             t_job(pick(s, t_at, [g for g in t_jobs for _ in (0, 1)]), n)
 
+        @pl.when(functools.reduce(jnp.logical_or, [s == at for at in x_at]))
+        def _():
+            x_send(pick(s, x_at, t_jobs))
+
         for at, job in (
-            (late + 3, x_send), (late + 3 + 4 * UNIT, x_sum), (late + 3 + 7 * UNIT, out_planes),
+            (late + 3 + 4 * UNIT, x_sum), (late + 3 + 7 * UNIT, out_planes),
             (late + 3 + 10 * UNIT, out_spread),
         ):
             pl.when(s == at)(job)

time: 128 us -> 128 us (level)
  the two profiles are of different devices: /device:TPU:64 before, /device:TPU:16 now
where the time goes in v6:
time: 128 us
  Pallas kernels  127 us (99%)
    pallas_call x1, Pallas kernels, per_device(): pl.pallas_call(kernel, out_shape=(jax.ShapeDtypeStruct((4, tok, quarter),...  125 us

profile of v6, /device:TPU:16, one launch (start us, length us, event | category | flops | bytes accessed | tf_op | source)
XLA Modules:
  0.0 127.6 jit_solution(6693617487638623341)
XLA Ops:
  0.6 124.8 %backward.1 = (bf16[4,96,256]{2,1,0:T(8,128)(2,1)}, bf16[256,1792]{1,0:T(8,128)(2,1)}) custom-call(bf16[96,1024]{1,0:T(8,128)(2,1)} %inp.1, bf16[192,1792]{1,0:T(8,128)(2,1)} %og.1, bf16[256,1792]{1,0:T(8,128)(2,1)} %wt.1), custom_call_target="tpu_custom_call" | custom-call | flops 5637144576 | bytes 4194304 | tf_op jit(solution)/shard_map/backward/pallas_call | solution.py:520
  125.4 2.2 %place.1 = (bf16[96,1024]{1,0:T(8,128)(2,1)}, bf16[256,1792]{1,0:T(8,128)(2,1)}) custom-call(bf16[4,96,256]{2,1,0:T(8,128)(2,1)} %get-tuple-element.4.parts, bf16[256,1792]{1,0:T(8,128)(2,1)} %get-tuple-element.5.shard), custom_call_target="tpu_custom_call" | custom-call | tf_op jit(solution)/shard_map/place/pallas_call | solution.py:558
